TPU v7x, 256 devices: a whole 4x4x8 slice. The times are simulated.
256 devices in a mesh: lat: 4 (over x_hi, core), lon: 64 (over z, y, x_lo).
Axes of the slice: x: 4 (x_hi: 2, x_lo: 2; x = x_hi * 2 + x_lo), y: 4, z: 8, core: 2. Of those that a mesh axis runs over, the one named last changes fastest.
Arguments:
- tokens: bfloat16 [2, 24, 768, 1024], P(None, 'lat', 'lon'), may hold values from -6 to 6
- cotangent: bfloat16 [2, 24, 768, 1024], P(None, 'lat', 'lon'), may hold values from -16 to 16
- qkv_weight: bfloat16 [1024, 3072], replicated, may hold values from -0.1875 to 0.1875
- out_weight: bfloat16 [1024, 1024], replicated, may hold values from -0.1875 to 0.1875
- bias_table: float32 [759, 16], replicated, may hold values from -12 to 332
- rel_index: int32 [144, 144], replicated, may hold values from 0 to 758
Outputs:
- token_grad: bfloat16 [2, 24, 768, 1024], P(None, 'lat', 'lon')
- out_grad: float32 [1024, 1024], P('lat', 'lon')
- table_grad: float32 [759, 16], replicated
All inputs are finite; a program needn't handle non-finite values.
Results may differ from a plain program's by a relative error of at most 0.013.
Values may be sent and summed in bfloat16 or wider, within the bound.
No kernel may reach another device: no remote copies, remote signals or barrier semaphores. Data moves between devices by JAX's collectives and lax.ppermute only.
A program may use at most 128 MiB of HBM per device.

v0:
```python
import jax
import jax.numpy as jnp
from jax import lax
from jax.sharding import PartitionSpec as P

WLAT = 6
WLON = 12


def from_behind(array, axis, by):
    peers = lax.axis_size(axis)
    return lax.ppermute(array, axis, [(i, (i + by) % peers) for i in range(peers)])


def to_windows(field_block, lat_win, lon_win):
    level_count = field_block.shape[0]
    lat_rows = field_block.shape[1]
    lon_cols = field_block.shape[2]
    trailing = field_block.shape[3:]
    shaped = field_block.reshape(
        (level_count, lat_rows // lat_win, lat_win, lon_cols // lon_win, lon_win) + trailing
    )
    order_axes = (1, 3, 0, 2, 4) + tuple(range(5, 5 + len(trailing)))
    return shaped.transpose(order_axes).reshape((-1, level_count * lat_win * lon_win) + trailing)


def from_windows(windows, level_count, lat_rows, lon_cols, lat_win, lon_win):
    features = windows.shape[-1]
    shaped = windows.reshape(
        lat_rows // lat_win, lon_cols // lon_win, level_count, lat_win, lon_win, features
    )
    return shaped.transpose(2, 0, 3, 1, 4, 5).reshape(level_count, lat_rows, lon_cols, features)


def index_blocks(rel_index):
    win_tokens = rel_index.shape[0]
    block_rows = 16
    return rel_index.reshape(win_tokens // block_rows, block_rows * win_tokens)


def one_hot_block(index_row, table_rows):
    return (index_row[:, None] == jnp.arange(table_rows, dtype=jnp.int32)[None, :]).astype(
        jnp.float32
    )


def lookup_bias(bias_table, rel_index):
    win_tokens = rel_index.shape[0]
    table_rows, head_count = bias_table.shape

    def lookup_step(carry_state, index_row):
        picked = jnp.dot(
            one_hot_block(index_row, table_rows), bias_table, precision=lax.Precision.HIGHEST
        )
        return (carry_state, picked)

    unused, looked = lax.scan(lookup_step, jnp.zeros((), jnp.float32), index_blocks(rel_index))
    return jnp.transpose(looked.reshape(win_tokens, win_tokens, head_count), (2, 0, 1))


def table_sums(score_local, rel_index, table_rows):
    head_count = score_local.shape[0]
    blocks = index_blocks(rel_index)
    pieces = jnp.transpose(score_local, (1, 2, 0)).reshape(
        blocks.shape[0], blocks.shape[1], head_count
    )

    def table_step(total, inputs):
        index_row, piece = inputs
        term = lax.dot_general(
            one_hot_block(index_row, table_rows),
            piece,
            (((0,), (0,)), ((), ())),
            precision=lax.Precision.HIGHEST,
            preferred_element_type=jnp.float32,
        )
        return (total + term, None)

    total, unused = lax.scan(
        table_step, jnp.zeros((table_rows, head_count), jnp.float32), (blocks, pieces)
    )
    return total


def body(tokens, cotangent, qkv_weight, out_weight, bias_table, rel_index):
    level_count, lat_rows, lon_cols, features = tokens.shape
    half_lat = WLAT // 2
    half_lon = WLON // 2
    rim_tokens, rim_cot = from_behind(
        (tokens[:, :, :half_lon], cotangent[:, :, :half_lon]), "lon", -1
    )
    wide_tokens = jnp.concatenate([tokens[:, :, half_lon:], rim_tokens], axis=2)
    wide_cot = jnp.concatenate([cotangent[:, :, half_lon:], rim_cot], axis=2)
    upper_tokens, upper_cot = from_behind(
        (wide_tokens[:, :half_lat], wide_cot[:, :half_lat]), "lat", -1
    )
    moved_tokens = jnp.concatenate([wide_tokens[:, half_lat:], upper_tokens], axis=1)
    moved_cot = jnp.concatenate([wide_cot[:, half_lat:], upper_cot], axis=1)
    row_ids = jnp.arange(lat_rows, dtype=jnp.int32)
    last_slab = lax.axis_index("lat") == lax.axis_size("lat") - 1
    wrapped = jnp.logical_and(last_slab, row_ids >= lat_rows - half_lat).astype(jnp.int32)
    wrapped = jnp.broadcast_to(wrapped[None, :, None], (level_count, lat_rows, lon_cols))
    tok_windows = to_windows(moved_tokens, WLAT, WLON)
    win_count = tok_windows.shape[0]
    win_tokens = tok_windows.shape[1]
    cot_flat = to_windows(moved_cot, WLAT, WLON).reshape(-1, features)
    wrap_windows = to_windows(wrapped, WLAT, WLON)
    allowed = wrap_windows[:, :, None] == wrap_windows[:, None, :]
    bias = lookup_bias(bias_table, rel_index)
    head_count = bias.shape[0]
    head_size = features // head_count
    scaling = head_size ** (-0.5)
    as_float = tok_windows.reshape(-1, features).astype(jnp.float32)
    centred = as_float - jnp.mean(as_float, axis=1, keepdims=True)
    inv_std = lax.rsqrt(jnp.mean(centred * centred, axis=1, keepdims=True) + 1e-05)
    normed = centred * inv_std
    hidden = normed.astype(jnp.bfloat16)
    projected = jnp.dot(hidden, qkv_weight, preferred_element_type=jnp.float32).astype(jnp.bfloat16)

    def split_heads(values):
        return values.reshape(win_count, win_tokens, head_count, head_size)

    query_heads = split_heads(projected[:, :features])
    key_heads = split_heads(projected[:, features : 2 * features])
    value_heads = split_heads(projected[:, 2 * features :])
    scores = (
        jnp.einsum("nihd,njhd->nhij", query_heads, key_heads, preferred_element_type=jnp.float32)
        * scaling
        + bias[None]
    )
    scores = jnp.where(allowed[:, None], scores, -jnp.inf)
    row_max = jnp.max(scores, axis=3, keepdims=True)
    expo = jnp.exp(scores - row_max)
    probs = expo / jnp.sum(expo, axis=3, keepdims=True)
    probs_half = probs.astype(jnp.bfloat16)
    attended = (
        jnp.einsum("nhij,njhd->nihd", probs_half, value_heads, preferred_element_type=jnp.float32)
        .astype(jnp.bfloat16)
        .reshape(-1, features)
    )
    grad_att = lax.dot_general(
        cot_flat, out_weight, (((1,), (1,)), ((), ())), preferred_element_type=jnp.float32
    ).astype(jnp.bfloat16)
    grad_heads = split_heads(grad_att)
    grad_probs = jnp.einsum(
        "nihd,njhd->nhij", grad_heads, value_heads, preferred_element_type=jnp.float32
    )
    grad_values = jnp.einsum(
        "nhij,nihd->njhd", probs_half, grad_heads, preferred_element_type=jnp.float32
    ).astype(jnp.bfloat16)
    grad_scores = probs * (grad_probs - jnp.sum(probs * grad_probs, axis=3, keepdims=True))
    scaled_half = (grad_scores * scaling).astype(jnp.bfloat16)
    grad_query = jnp.einsum(
        "nhij,njhd->nihd", scaled_half, key_heads, preferred_element_type=jnp.float32
    ).astype(jnp.bfloat16)
    grad_key = jnp.einsum(
        "nhij,nihd->njhd", scaled_half, query_heads, preferred_element_type=jnp.float32
    ).astype(jnp.bfloat16)
    stacked = jnp.concatenate(
        [
            grad_query.reshape(-1, features),
            grad_key.reshape(-1, features),
            grad_values.reshape(-1, features),
        ],
        axis=1,
    )
    grad_normed = lax.dot_general(
        stacked, qkv_weight, (((1,), (1,)), ((), ())), preferred_element_type=jnp.float32
    )
    branch = (
        grad_normed
        - jnp.mean(grad_normed, axis=1, keepdims=True)
        - normed * jnp.mean(grad_normed * normed, axis=1, keepdims=True)
    ) * inv_std
    grad_flat = (cot_flat.astype(jnp.float32) + branch).astype(jnp.bfloat16)
    grad_moved = from_windows(
        grad_flat.reshape(win_count, win_tokens, features),
        level_count,
        lat_rows,
        lon_cols,
        WLAT,
        WLON,
    )
    lower_part = from_behind(grad_moved[:, -half_lat:], "lat", 1)
    lat_fixed = jnp.concatenate([lower_part, grad_moved[:, :-half_lat]], axis=1)
    left_part = from_behind(lat_fixed[:, :, -half_lon:], "lon", 1)
    token_grad = jnp.concatenate([left_part, lat_fixed[:, :, :-half_lon]], axis=2)
    score_local = jnp.sum(grad_scores, axis=0)
    local_table = table_sums(score_local, rel_index, bias_table.shape[0])
    table_grad = lax.psum(local_table, ("lat", "lon"))
    row_block = lax.psum_scatter(
        lax.dot_general(
            attended, cot_flat, (((0,), (0,)), ((), ())), preferred_element_type=jnp.float32
        ).astype(jnp.bfloat16),
        "lat",
        scatter_dimension=0,
        tiled=True,
    ).astype(jnp.float32)
    out_grad = lax.psum_scatter(row_block, "lon", scatter_dimension=1, tiled=True)
    return (token_grad, out_grad, table_grad)


def solution(mesh):
    return jax.shard_map(
        body,
        mesh=mesh,
        in_specs=(P(None, "lat", "lon", None), P(None, "lat", "lon", None), P(), P(), P(), P()),
        out_specs=(P(None, "lat", "lon", None), P("lat", "lon"), P()),
        check_vma=False,
    )
```

profile of v0, /device:TPU:6, one launch (start us, length us, event | category | flops | bytes accessed | tf_op | source)
XLA Modules:
  0.0 488.5 jit_solution(13839528370461952158)
XLA Ops:
  7.2 1.3 fusion.39
  9.5 1.2 fusion.40
  10.7 9.0 %collective-permute-start = (bf16[2,6,6,1024]{3,0,2,1:T(2,128)(2,1)S(1)}, bf16[2,6,6,1024]{3,0,2,1:T(2,128)(2,1)S(1)}, u32[]{:S(2)}, u32[]{:S(2)}) collective-permute-start(bf16[2,6,6,1024]{3,0,2,1:T(2,128)(2,1)S(1)} %get-tuple-element.120), channel_id=1, source_target_pairs={{0,63},{1,0},{2,1},{3,2},{4,3},{5,4},{6,5},{7,6},{8,7},{9,8},{10,9... | collective-permute-start | bytes 442376 | tf_op jit(solution)/shard_map/ppermute | solution.py:12
  20.7 71.4 %while.21 = (s32[]{:T(128)}, f32[9,2304,16]{1,0,2:T(8,128)}, s32[9,2304]{1,0:T(8,128)S(1)}, f32[759,16]{0,1:T(8,128)}, s32[]{:T(128)}, /*index=5*/s32[]{:T(128)}) while((s32[]{:T(128)}, f32[9,2304,16]{1,0,2:T(8,128)}, s32[9,2304]{1,0:T(8,128)S(1)}, f32[759,16]{0,1:T(8,128)}, s32[]{:T(128)}, /*index=5*/s32[]{:T(128)}) %tuple.59), condition=%wide.region_3.4_spmd, body=%wide.region_2.3_spmd.sunk | while | flops 337506048 | bytes 813581 | solution.py:57
  20.8 4.1 fusion.62
  25.0 3.6 dynamic_update_slice.5
  28.7 4.1 fusion.62
  33.0 3.6 dynamic_update_slice.5
  36.6 4.1 fusion.62
  40.9 3.6 dynamic_update_slice.5
  44.6 4.1 fusion.62
  48.8 3.6 dynamic_update_slice.5
  52.5 4.1 fusion.62
  56.8 3.6 dynamic_update_slice.5
  60.5 4.1 fusion.62
  64.7 3.6 dynamic_update_slice.5
  68.4 4.1 fusion.62
  72.6 3.6 dynamic_update_slice.5
  76.3 4.1 fusion.62
  80.6 3.6 dynamic_update_slice.5
  84.3 4.1 fusion.62
  88.5 3.6 dynamic_update_slice.5
  93.2 4.0 reshape.205
  97.2 3.5 copy.81
  100.7 1.1 fusion.29
  101.8 1.2 collective-permute-start.1
  105.1 3.9 convolution_convert_fusion
  109.9 1.2 copy.103
  111.0 2.0 copy.104
  114.0 1.4 pad_maximum_fusion.1
  116.2 1.1 reshape_reshape_transpose_reshape.4
  117.3 3.9 fusion.35
  123.2 2.0 convolution_convert_fusion.1
  125.3 1.6 convolution_convert_fusion.6
  126.9 2.0 copy.105
  128.8 2.9 multiply_reduce_fusion
  135.4 1.2 slice-done
  137.3 2.4 fusion.34
  140.5 5.3 %fusion.6 = f32[144,144,16]{0,1,2:T(8,128)} fusion(f32[16,144,144]{1,2,0:T(8,128)} %copy-done.3, f32[144,144,16]{0,1,2:T(8,128)} %copy.81, f32[16,144,144]{1,2,0:T(8,128)} %get-tuple-element.121, f32[144,16]{0,1:T(8,128)S(1)} %bitcast.98, f32[144,16]{0,1:T(8,128)S(1)} %bitcast.97, f32[144,16]{0,1:T(8,128)S(1)} %bitcast.96, ...), kind=kLoop, calls=%fused_computation.14 | loop fusion | flops 2322432 | bytes 5356800 | tf_op jit(solution)/shard_map/mul | solution.py:151
  145.9 3.5 copy.93
  149.4 4.0 reshape.212
  153.6 12.4 %reduce-scatter.5.cloned.1.call-done = bf16[256,1024]{1,0:T(8,128)(2,1)} async-done(((bf16[1024,1024]{1,0:T(8,128)(2,1)}), bf16[256,1024]{1,0:T(8,128)(2,1)}) %reduce-scatter.5.cloned.1.call-update) | async-done | bytes 524304 | tf_op jit(solution)/shard_map/reduce_scatter | solution.py:191
  165.9 2.2 copy.101
  168.2 39.5 %while.22 = (s32[]{:T(128)}, f32[759,16]{0,1:T(8,128)S(1)}, s32[9,2304]{1,0:T(8,128)}, f32[9,2304,16]{1,0,2:T(8,128)}, s32[]{:T(128)}, /*index=5*/s32[]{:T(128)}) while((s32[]{:T(128)}, f32[759,16]{0,1:T(8,128)S(1)}, s32[9,2304]{1,0:T(8,128)}, f32[9,2304,16]{1,0,2:T(8,128)}, s32[]{:T(128)}, /*index=5*/s32[]{:T(128)}) %tuple.70), condition=%wide.region_12.13_spmd.clone, body=%wide.region_11.12_spmd.clone.sunk | while | flops 337530336 | bytes 567255 | solution.py:79
  168.2 1.4 constant_dynamic-slice_fusion.2
  170.5 2.1 fusion.63
  172.6 1.4 constant_dynamic-slice_fusion.2
  174.9 2.1 fusion.63
  177.0 1.4 constant_dynamic-slice_fusion.2
  179.3 2.1 fusion.63
  181.4 1.4 constant_dynamic-slice_fusion.2
  183.7 2.1 fusion.63
  185.8 1.4 constant_dynamic-slice_fusion.2
  188.1 2.1 fusion.63
  190.1 1.4 constant_dynamic-slice_fusion.2
  192.5 2.1 fusion.63
  194.5 1.4 constant_dynamic-slice_fusion.2
  196.8 2.1 fusion.63
  198.9 1.4 constant_dynamic-slice_fusion.2
  201.2 2.1 fusion.63
  203.3 1.4 constant_dynamic-slice_fusion.2
  205.6 2.1 fusion.63
  207.7 79.5 %psum.7 = f32[759,16]{0,1:T(8,128)} all-reduce(f32[759,16]{0,1:T(8,128)S(1)} %get-tuple-element.48), channel_id=1, replica_groups=mesh['lat'=4,'lon'=64] {'lat','lon'}, use_global_device_ids=true, to_apply=%region_13.14 | all-reduce | flops 12144 | bytes 97152 | tf_op jit(solution)/shard_map/psum | solution.py:190
  288.3 193.3 %reduce-scatter.7.cloned.1.call-done = f32[16,256]{1,0:T(8,128)} async-done(((f32[1024,256]{1,0:T(8,128)}), f32[16,256]{1,0:T(8,128)}) %reduce-scatter.7.cloned.1.call-update) | async-done | bytes 16400
  (114 shorter events, 26.4 us)
Async XLA Ops:
  7.2 118.1 %copy-start = (bf16[1024,1024]{1,0:T(8,128)(2,1)S(1)}, bf16[1024,1024]{1,0:T(8,128)(2,1)}, u32[]{:S(2)}) copy-start(bf16[1024,1024]{1,0:T(8,128)(2,1)} %param.13) | copy-start | bytes 6291460
  7.2 158.7 %reduce-scatter.5.cloned.1.call-start = ((), (), s32[]{:S(2)}) async-start(), calls=%async_computation.2 | async-start | bytes 2621440 | tf_op jit(solution)/shard_map/reduce_scatter | solution.py:191
  8.6 83.8 %collective-permute-start.2 = (bf16[2,6,6,1024]{3,0,2,1:T(2,128)(2,1)S(1)}, bf16[2,6,6,1024]{3,0,2,1:T(2,128)(2,1)S(1)}, u32[]{:S(2)}, u32[]{:S(2)}) collective-permute-start(bf16[2,6,6,1024]{3,0,2,1:T(2,128)(2,1)S(1)} %get-tuple-element.116), channel_id=1, source_target_pairs={{0,63},{1,0},{2,1},{3,2},{4,3},{5,4},{6,5},{7,6},{8,7},{9,8},{10,9... | collective-permute-start | bytes 442376 | tf_op jit(solution)/shard_map/ppermute | solution.py:12
  10.7 90.0 %collective-permute-start = (bf16[2,6,6,1024]{3,0,2,1:T(2,128)(2,1)S(1)}, bf16[2,6,6,1024]{3,0,2,1:T(2,128)(2,1)S(1)}, u32[]{:S(2)}, u32[]{:S(2)}) collective-permute-start(bf16[2,6,6,1024]{3,0,2,1:T(2,128)(2,1)S(1)} %get-tuple-element.120), channel_id=1, source_target_pairs={{0,63},{1,0},{2,1},{3,2},{4,3},{5,4},{6,5},{7,6},{8,7},{9,8},{10,9... | collective-permute-start | bytes 442376 | tf_op jit(solution)/shard_map/ppermute | solution.py:12
  92.2 5.1 %copy-start.7 = (s32[9,2304]{1,0:T(8,128)}, s32[9,2304]{1,0:T(8,128)S(1)}, u32[]{:S(2)}) copy-start(s32[9,2304]{1,0:T(8,128)S(1)} %get-tuple-element.222) | copy-start | bytes 248836
  92.7 10.3 %collective-permute-start.3 = (bf16[2,3,12,1024]{3,0,2,1:T(2,128)(2,1)S(1)}, bf16[2,3,12,1024]{3,0,2,1:T(2,128)(2,1)S(1)}, u32[]{:S(2)}, u32[]{:S(2)}) collective-permute-start(bf16[2,3,12,1024]{3,0,2,1:T(2,128)(2,1)S(1)} %get-tuple-element.114), channel_id=1, source_target_pairs={{0,192},{64,0},{128,64},{192,128},{1,193},{65,1},{129,65},{193,129... | collective-permute-start | bytes 442376 | tf_op jit(solution)/shard_map/ppermute | solution.py:12
  101.8 12.2 %collective-permute-start.1 = (bf16[2,3,12,1024]{3,0,2,1:T(2,128)(2,1)}, bf16[2,3,12,1024]{3,0,2,1:T(2,128)(2,1)}, u32[]{:S(2)}, u32[]{:S(2)}) collective-permute-start(bf16[2,3,12,1024]{3,0,2,1:T(2,128)(2,1)} %get-tuple-element.118), channel_id=1, source_target_pairs={{0,192},{64,0},{128,64},{192,128},{1,193},{65,1},{129,65},{193,129... | collective-permute-start | bytes 442376 | tf_op jit(solution)/shard_map/ppermute | solution.py:12
  121.2 2.0 copy-start.1
  121.2 2.0 copy-start.8
  121.2 1.4 copy-start.5
  121.6 1.6 copy-start.11
  125.2 356.4 %reduce-scatter.7.cloned.1.call-start = ((), (), s32[]{:S(2)}) async-start(), calls=%async_computation.3 | async-start | bytes 1064960
  128.8 3.5 copy-start.2
  128.8 3.5 copy-start.9
  128.8 3.5 copy-start.12
  131.7 0.6 copy-start.14
  131.7 1.4 copy-start.3
  133.2 1.1 copy-start.4
  133.2 1.6 copy-start.6
  134.2 2.4 slice-start
  134.8 2.6 slice-start.1
  139.8 0.8 copy-start.10
  139.8 0.8 copy-start.13
  139.8 0.8 copy-start.15
  140.2 13.2 %collective-permute-start.4 = (bf16[2,3,12,1024]{3,2,1,0:T(8,128)(2,1)S(1)}, bf16[2,3,12,1024]{3,2,1,0:T(8,128)(2,1)S(1)}, u32[]{:S(2)}, u32[]{:S(2)}) collective-permute-start(bf16[2,3,12,1024]{3,2,1,0:T(8,128)(2,1)S(1)} %get-tuple-element.111), channel_id=1, source_target_pairs={{0,64},{64,128},{128,192},{192,0},{1,65},{65,129},{129,193},{193,1... | collective-permute-start | bytes 442376 | tf_op jit(solution)/shard_map/ppermute | solution.py:12
  153.4 14.8 %copy-start.16 = (f32[759,16]{0,1:T(8,128)S(1)}, f32[759,16]{0,1:T(8,128)}, u32[]{:S(2)}) copy-start(f32[759,16]{0,1:T(8,128)} %custom-call) | copy-start | bytes 145732
  153.5 133.7 %collective-permute-start.5 = (bf16[2,6,6,1024]{3,2,1,0:T(8,128)(2,1)S(1)}, bf16[2,6,6,1024]{3,2,1,0:T(8,128)(2,1)S(1)}, u32[]{:S(2)}, u32[]{:S(2)}) collective-permute-start(bf16[2,6,6,1024]{3,2,1,0:T(8,128)(2,1)S(1)} %fusion.27), channel_id=1, source_target_pairs={{0,1},{1,2},{2,3},{3,4},{4,5},{5,6},{6,7},{7,8},{8,9},{9,10},{10,1... | collective-permute-start | bytes 442376 | tf_op jit(solution)/shard_map/ppermute | solution.py:12
Sparse Core Ops, SparseCore 0:
  125.4 40.5 reduce-scatter.4
  169.1 312.4 reduce-scatter.6
where the time goes:
time: 496 us; the launch traced here: 489 us
  waiting for transfers between devices  206 us (42%)
  local copies, waits for them, and re-layouts  91.6 us (18%)
  blocking collectives  79.5 us (16%)
  matrix products  73.8 us (15%)
  between operations  14.4 us (3%)
  starting transfers between devices  12 us (2%)
  other arithmetic  11.2 us (2%)
    unnamed x3, waiting for transfers between devices  193 us
    psum x1, blocking collectives, body(): table_grad = lax.psum(local_table, ('lat', 'lon'))  79.5 us
    dot_general x9, matrix products, lookup_step(): jnp.dot(one_hot_block(index_row, table_rows), bias_table, precision=lax.P...  36.6 us
    dynamic_update_slice x18, local copies, waits for them, and re-layouts, lookup_bias(): lax.scan(lookup_step, jnp.zeros((), jnp.float32), index_blocks(rel_index))  34.5 us
    dot_general x9, matrix products, table_step(): lax.dot_general(one_hot_block(index_row, table_rows), piece, (((0,), (0,)...  18.6 us
    dynamic_slice x9, local copies, waits for them, and re-layouts, table_sums(): lax.scan(table_step, jnp.zeros((table_rows, head_count), jnp.float32), (b...  12.4 us
    reduce_scatter x1, waiting for transfers between devices, body(): lax.psum_scatter(lax.dot_general(attended, cot_flat, (((0,), (0,)), ((),...  12.4 us
    ppermute x6, starting transfers between devices, from_behind(): lax.ppermute(array, axis, [(i, (i + by) % peers) for i in range(peers)])  11.9 us
  transfers between devices with their start and end apart: 8, of which 2 were waited for; matrix products, arithmetic and copies ran while one was open for 33% of the time, Pallas kernels for 0%

commit v1 on v0

v1 whole, which is shorter than its diff:
```python
import functools

import jax
import jax.numpy as jnp
from jax import lax
from jax.experimental import pallas as pl
from jax.experimental.pallas import tpu as pltpu
from jax.sharding import Mesh
from jax.sharding import PartitionSpec as P

LEVELS = 2
WLAT = 6
WLON = 12
HALF_LAT = WLAT // 2
HALF_LON = WLON // 2
WIN = LEVELS * WLAT * WLON
PIECE = WIN // 4
HEADS = 16
HEAD = 64
D = HEADS * HEAD
NREL = 759
ROWS = 768
SCALE = HEAD ** (-0.5)
BF = jnp.bfloat16
F32 = jnp.float32
VMEM = pl.BlockSpec(memory_space=pltpu.VMEM)
ANY = pl.BlockSpec(memory_space=pl.ANY)
SMEM = pl.BlockSpec(memory_space=pltpu.SMEM)
LAT = ("xh", "core")
LON = ("z", "y", "xl")
NEAR = ("core", "y", "xl")
FAR = ("xh", "z")
ALL = ("xh", "core", "z", "y", "xl")

NT = (((1,), (1,)), ((), ()))
TN = (((0,), (0,)), ((), ()))


def dot(a, b, dims=(((1,), (0,)), ((), ()))):
    return lax.dot_general(a, b, dims, preferred_element_type=F32)


def params(mib):
    return pltpu.CompilerParams(vmem_limit_bytes=mib * 1024 * 1024)


def cost(flops, moved):
    return pl.CostEstimate(flops=flops, bytes_accessed=moved, transcendentals=0)


def groups():
    for level in range(LEVELS):
        for row in range(HALF_LAT):
            yield level, row, (level * HALF_LAT + row) * HALF_LON


def pack_kernel(tok, cot, lon_o, lat_o, dia_o, lon_s, lat_s, dia_s):
    for half, src in enumerate((tok, cot)):
        for level, row, at in groups():
            at = half * PIECE + at
            low = src[level, row].astype(F32)
            high = src[level, row + HALF_LAT].astype(F32)
            lon_s[at : at + HALF_LON] = high[:HALF_LON]
            dia_s[at : at + HALF_LON] = low[:HALF_LON]
            lat_s[at : at + HALF_LON] = low[HALF_LON:]
    lon_o[...] = lon_s[...].astype(BF)
    lat_o[...] = lat_s[...].astype(BF)
    dia_o[...] = dia_s[...].astype(BF)


def pack(tokens, cotangent):
    out = jax.ShapeDtypeStruct((2 * PIECE, D), BF)
    return pl.pallas_call(
        pack_kernel,
        out_shape=(out, out, out),
        in_specs=[VMEM, VMEM],
        out_specs=(VMEM, VMEM, VMEM),
        scratch_shapes=[pltpu.VMEM((2 * PIECE, D), F32)] * 3,
        compiler_params=params(16),
        name="pack",
    )(tokens, cotangent)


def bias_kernel(last, table, rel, out):
    row = lax.broadcasted_iota(jnp.int32, (WIN, 256), 0)
    col = lax.broadcasted_iota(jnp.int32, (WIN, 256), 1)
    half = WIN // 2
    split = (lax.rem(row, half) >= half // 2) == (lax.rem(col, half) >= half // 2)
    allowed = jnp.logical_or(split, last[0] == 0)
    index = rel[...]
    low = index & 127
    high = index >> 7

    def one_head(head, carry):
        line = table[pl.ds(head, 1), :]
        halves = []
        for side in (0, 1):
            lanes = slice(side * 128, side * 128 + 128)
            total = jnp.zeros((WIN, 128), F32)
            for part in range(ROWS // 128):
                source = jnp.broadcast_to(line[:, part * 128 : part * 128 + 128], (WIN, 128))
                found = jnp.take_along_axis(
                    source, low[:, lanes], axis=1, mode="promise_in_bounds"
                )
                total = jnp.where(high[:, lanes] == part, found, total)
            halves.append(jnp.where(allowed[:, lanes], total, -jnp.inf))
        out[head, :, :128] = halves[0]
        out[head, :, 128:] = halves[1][:, : WIN - 128]
        return carry

    lax.fori_loop(0, HEADS, one_head, 0)


def bias_of(last, table, rel):
    return pl.pallas_call(
        bias_kernel,
        out_shape=jax.ShapeDtypeStruct((HEADS, WIN, WIN), F32),
        in_specs=[SMEM, VMEM, VMEM],
        out_specs=VMEM,
        compiler_params=params(16),
        cost_estimate=cost(10_000_000, 4_000_000),
        name="bias",
    )(last, table, rel)


def gather_window(out, own, lon, lat, dia, offset):
    for level, row, at in groups():
        at = at + offset
        base = level * WLAT * WLON + row * WLON
        out[base : base + HALF_LON] = own[level, row + HALF_LAT].astype(F32)[HALF_LON:]
        out[base + HALF_LON : base + WLON] = lon[at : at + HALF_LON]
        base = base + HALF_LAT * WLON
        out[base : base + HALF_LON] = lat[at : at + HALF_LON]
        out[base + HALF_LON : base + WLON] = dia[at : at + HALF_LON]


def forward_kernel(
    tok, cot, lon, lat, dia, bias, wqkv_hbm, wout_hbm,
    cot_o, att_o, proj_o, gatt_o, ph_o, ds_o, g_o, normed_o, std_o,
    x_s, c_s, lon_s, lat_s, dia_s, wqkv, wout, sems,
):
    copies = [pltpu.make_async_copy(wout_hbm, wout, sems.at[3])]
    copies += [
        pltpu.make_async_copy(
            wqkv_hbm.at[:, pl.ds(part * D, D)], wqkv.at[part], sems.at[part]
        )
        for part in range(3)
    ]
    for copy in copies:
        copy.start()
    lon_s[...] = lon[...].astype(F32)
    lat_s[...] = lat[...].astype(F32)
    dia_s[...] = dia[...].astype(F32)
    gather_window(c_s, cot, lon_s, lat_s, dia_s, PIECE)
    gather_window(x_s, tok, lon_s, lat_s, dia_s, 0)
    cot_flat = c_s[...].astype(BF)
    cot_o[...] = cot_flat
    copies[0].wait()
    gatt_o[...] = dot(cot_flat, wout[...], NT).astype(BF)
    x = x_s[...]
    centred = x - jnp.mean(x, axis=1, keepdims=True)
    inv_std = lax.rsqrt(jnp.mean(centred * centred, axis=1, keepdims=True) + 1e-05)
    normed = centred * inv_std
    normed_o[...] = normed
    std_o[...] = jnp.broadcast_to(inv_std, (WIN, 128))
    hidden = normed.astype(BF)
    for part in range(3):
        copies[1 + part].wait()
        proj_o[part] = dot(hidden, wqkv[part]).astype(BF)
    lane = lax.broadcasted_iota(jnp.int32, (WIN, 128), 1)
    masks = (lane < HEAD, lane >= HEAD)
    zero = jnp.zeros((WIN, 128), BF)

    for pair in range(HEADS // 2):
        lanes = slice(pair * 128, pair * 128 + 128)
        query = proj_o[0, :, lanes]
        key = proj_o[1, :, lanes]
        value = proj_o[2, :, lanes]
        grad = gatt_o[:, lanes]
        attended = []
        for side in (0, 1):
            head = pair * 2 + side
            scores = dot(jnp.where(masks[side], query, zero), key, NT) * SCALE + bias[head]
            expo = jnp.exp(scores - jnp.max(scores, axis=1, keepdims=True))
            probs = expo * (1.0 / jnp.sum(expo, axis=1, keepdims=True))
            half = probs.astype(BF)
            ph_o[head] = half
            attended.append(dot(half, value))
            grad_probs = dot(jnp.where(masks[side], grad, zero), value, NT)
            inner = jnp.sum(probs * grad_probs, axis=1, keepdims=True)
            grad_scores = probs * (grad_probs - inner)
            g_o[head] = grad_scores
            ds_o[head] = (grad_scores * SCALE).astype(BF)
        block, core = pair // 4, (pair // 2) % 2
        at = block * 256 + (pair % 2) * 128
        att_o[core, :, at : at + 128] = jnp.where(masks[0], attended[0], attended[1]).astype(BF)


def forward(tokens, cotangent, lon, lat, dia, bias, qkv_weight, out_weight):
    square = (HEADS, WIN, WIN)
    return pl.pallas_call(
        forward_kernel,
        out_shape=(
            jax.ShapeDtypeStruct((WIN, D), BF),
            jax.ShapeDtypeStruct((2, WIN, D // 2), BF),
            jax.ShapeDtypeStruct((3, WIN, D), BF),
            jax.ShapeDtypeStruct((WIN, D), BF),
            jax.ShapeDtypeStruct(square, BF),
            jax.ShapeDtypeStruct(square, BF),
            jax.ShapeDtypeStruct(square, F32),
            jax.ShapeDtypeStruct((WIN, D), F32),
            jax.ShapeDtypeStruct((WIN, 128), F32),
        ),
        in_specs=[VMEM] * 6 + [ANY] * 2,
        out_specs=(VMEM,) * 9,
        scratch_shapes=[
            pltpu.VMEM((WIN, D), F32),
            pltpu.VMEM((WIN, D), F32),
            pltpu.VMEM((2 * PIECE, D), F32),
            pltpu.VMEM((2 * PIECE, D), F32),
            pltpu.VMEM((2 * PIECE, D), F32),
            pltpu.VMEM((3, D, D), BF),
            pltpu.VMEM((D, D), BF),
            pltpu.SemaphoreType.DMA((4,)),
        ],
        compiler_params=params(40),
        cost_estimate=cost(3_000_000_000, 24_000_000),
        name="forward",
    )(tokens, cotangent, lon, lat, dia, bias, qkv_weight, out_weight)


def table_kernel(grads, rel, out):
    blocks = ROWS // 256
    lane_id = lax.broadcasted_iota(jnp.int32, (256, WIN), 0)

    def one_row(i, total):
        index = rel[pl.ds(i, 1), :][:, :WIN]
        hot = jnp.where(lane_id == (index & 255), 1.0, 0.0).astype(BF)
        grad = grads[:, pl.ds(i, 1), :].reshape(HEADS, WIN)
        high = grad.astype(BF).astype(F32)
        both = jnp.concatenate([high, grad - high], axis=0)
        block = index >> 8
        picked = jnp.concatenate(
            [jnp.where(block == part, both, 0.0) for part in range(blocks)], axis=0
        ).astype(BF)
        return total + dot(picked, hot, NT)

    total = lax.fori_loop(
        0, WIN, one_row, jnp.zeros((blocks * 2 * HEADS, 256), F32), unroll=4
    )
    for part in range(blocks):
        at = part * 2 * HEADS
        out[part * HEADS : (part + 1) * HEADS] = (
            total[at : at + HEADS] + total[at + HEADS : at + 2 * HEADS]
        )


def table_of(grads, rel):
    return pl.pallas_call(
        table_kernel,
        out_shape=jax.ShapeDtypeStruct((ROWS // 256 * HEADS, 256), F32),
        in_specs=[VMEM, VMEM],
        out_specs=VMEM,
        compiler_params=params(24),
        cost_estimate=cost(3_000_000_000, 4_000_000),
        name="table",
    )(grads, rel)


def backward_kernel(
    ph, ds, proj, gatt, cot, normed, std, wqkv_hbm, own_o, lon_o, lat_o, dia_o,
    stacked, grad_s, piece_s, wqkv, sems,
):
    copies = [
        pltpu.make_async_copy(
            wqkv_hbm.at[:, pl.ds(part * D, D)], wqkv.at[part], sems.at[part]
        )
        for part in range(3)
    ]
    for copy in copies:
        copy.start()
    lane = lax.broadcasted_iota(jnp.int32, (WIN, 128), 1)
    first = lane < HEAD
    for pair in range(HEADS // 2):
        lanes = slice(pair * 128, pair * 128 + 128)
        query = proj[0, :, lanes]
        key = proj[1, :, lanes]
        grad = gatt[:, lanes]
        found = ([], [], [])
        for side in (0, 1):
            head = pair * 2 + side
            weights = ds[head]
            found[0].append(dot(weights, key))
            found[1].append(dot(weights, query, TN))
            found[2].append(dot(ph[head], grad, TN))
        for part in range(3):
            stacked[part, :, lanes] = jnp.where(first, *found[part]).astype(BF)
    total = jnp.zeros((WIN, D), F32)
    for part in range(3):
        copies[part].wait()
        total = total + dot(stacked[part], wqkv[part], NT)
    norm = normed[...]
    branch = (
        total
        - jnp.mean(total, axis=1, keepdims=True)
        - norm * jnp.mean(total * norm, axis=1, keepdims=True)
    ) * std[:, :1]
    grad_s[...] = cot[...].astype(F32) + branch
    for which, out in enumerate((own_o, lon_o, lat_o, dia_o)):
        shift = (which // 2) * HALF_LAT * WLON + (which % 2) * HALF_LON
        for level, row, at in groups():
            base = level * WLAT * WLON + row * WLON + shift
            piece_s[at : at + HALF_LON] = grad_s[base : base + HALF_LON]
        out[...] = piece_s[...].astype(BF)


def backward(ph, ds, proj, gatt, cot, normed, std, qkv_weight):
    piece = jax.ShapeDtypeStruct((PIECE, D), BF)
    return pl.pallas_call(
        backward_kernel,
        out_shape=(piece,) * 4,
        in_specs=[VMEM] * 7 + [ANY],
        out_specs=(VMEM,) * 4,
        scratch_shapes=[
            pltpu.VMEM((3, WIN, D), BF),
            pltpu.VMEM((WIN, D), F32),
            pltpu.VMEM((PIECE, D), F32),
            pltpu.VMEM((3, D, D), BF),
            pltpu.SemaphoreType.DMA((3,)),
        ],
        compiler_params=params(32),
        cost_estimate=cost(2_000_000_000, 16_000_000),
        name="backward",
    )(ph, ds, proj, gatt, cot, normed, std, qkv_weight)


def join_kernel(own, lon, lat, dia, out, own_s, lon_s, lat_s, dia_s, line):
    own_s[...] = own[...].astype(F32)
    lon_s[...] = lon[...].astype(F32)
    lat_s[...] = lat[...].astype(F32)
    dia_s[...] = dia[...].astype(F32)
    for level, row, at in groups():
        line[:HALF_LON] = dia_s[at : at + HALF_LON]
        line[HALF_LON:] = lat_s[at : at + HALF_LON]
        out[level, row] = line[...].astype(BF)
        line[:HALF_LON] = lon_s[at : at + HALF_LON]
        line[HALF_LON:] = own_s[at : at + HALF_LON]
        out[level, row + HALF_LAT] = line[...].astype(BF)


def join(own, lon, lat, dia):
    return pl.pallas_call(
        join_kernel,
        out_shape=jax.ShapeDtypeStruct((LEVELS, WLAT, WLON, D), BF),
        in_specs=[VMEM] * 4,
        out_specs=VMEM,
        scratch_shapes=[pltpu.VMEM((PIECE, D), F32)] * 4 + [pltpu.VMEM((WLON, D), F32)],
        compiler_params=params(16),
        name="join",
    )(own, lon, lat, dia)


def shift(array, axes, by):
    peers = lax.axis_size(axes)
    return lax.ppermute(array, axes, [(i, (i + by) % peers) for i in range(peers)])


def shift_both(array, by):
    lats, lons = lax.axis_size(LAT), lax.axis_size(LON)
    pairs = [
        (a * lons + b, ((a + by) % lats) * lons + (b + by) % lons)
        for a in range(lats)
        for b in range(lons)
    ]
    return lax.ppermute(array, ALL, pairs)


def pick(array, index, axis):
    return lax.dynamic_index_in_dim(array, index, axis, keepdims=False)


def shared_sum(array, axes):
    peers = lax.axis_size(axes)
    copies = jnp.broadcast_to(array[None], (peers,) + array.shape)
    return jnp.sum(lax.all_to_all(copies, axes, 0, 0, tiled=True), axis=0)


def reduce_out(cot, att):
    core = lax.axis_index("core")
    att_far = lax.ppermute(pick(att, 1 - core, 0), "core", [(0, 1), (1, 0)])
    cot_far = lax.ppermute(cot, "core", [(0, 1), (1, 0)])
    mine = jnp.concatenate([pick(att, core, 0), att_far], axis=0)
    partial = dot(jnp.concatenate([cot, cot_far], axis=0), mine, TN).astype(BF)

    zs, ys, xls, xhs = (lax.axis_size(name) for name in ("z", "y", "xl", "xh"))
    partial = partial.reshape(zs, ys, xls * 16, D // 2)
    me = lax.axis_index("y")
    total = pick(partial, me, 1).astype(F32)
    for by in range(1, ys):
        total = total + shift(pick(partial, (me + by) % ys, 1), "y", by).astype(F32)
    partial = total.astype(BF).reshape(zs, xls, 16, xhs, 256)

    xh, xl = lax.axis_index("xh"), lax.axis_index("xl")
    total = pick(pick(partial, xh, 3), xl, 1).astype(F32)
    for flip in range(1, 4):
        a, b = flip // 2, flip % 2
        piece = pick(pick(partial, xh ^ a, 3), xl ^ b, 1)
        pairs = [(i, i ^ flip) for i in range(4)]
        total = total + lax.ppermute(piece, ("xh", "xl"), pairs).astype(F32)
    partial = total.astype(BF)

    pieces = lax.all_to_all(partial, "z", 0, 0, tiled=True)
    return jnp.sum(pieces.astype(F32), axis=0).T


def body(tokens, cotangent, qkv_weight, out_weight, bias_table, rel_index):
    last = (lax.axis_index("xh") * 2 + lax.axis_index("core") == 3).astype(jnp.int32).reshape(1)
    send = pack(tokens, cotangent)
    lon = shift(send[0], LON, -1)
    lat = shift(send[1], LAT, -1)
    dia = shift_both(send[2], -1)
    table = jnp.pad(bias_table.T, ((0, 0), (0, ROWS - NREL)))
    rel = jnp.pad(rel_index, ((0, 0), (0, 256 - WIN)))
    bias = bias_of(last, table, rel)
    cot, att, proj, gatt, ph, ds, grads, normed, std = forward(
        tokens, cotangent, lon, lat, dia, bias, qkv_weight, out_weight
    )
    out_grad = reduce_out(cot, att)
    sums = table_of(grads, rel)
    sums = shared_sum(shared_sum(sums, NEAR), FAR)
    table_grad = sums.reshape(ROWS // 256, HEADS, 256).transpose(0, 2, 1).reshape(ROWS, HEADS)[:NREL]
    own, lon, lat, dia = backward(ph, ds, proj, gatt, cot, normed, std, qkv_weight)
    token_grad = join(own, shift(lon, LON, 1), shift(lat, LAT, 1), shift_both(dia, 1))
    return (token_grad, out_grad, table_grad)


def solution(mesh):
    fine = Mesh(mesh.devices.reshape(2, 2, 8, 4, 2), ALL)
    grid = P(None, LAT, LON, None)
    return jax.shard_map(
        body,
        mesh=fine,
        in_specs=(grid, grid, P(), P(), P(), P()),
        out_specs=(grid, P(LAT, LON), P()),
        check_vma=False,
    )
```

time: 496 us -> 138 us (0.28)
  the two profiles are of different devices: /device:TPU:6 before, /device:TPU:1 now
where the time goes in v1:
time: 138 us; the launch traced here: 137 us
  starting transfers between devices  40.4 us (29%)
  Pallas kernels  39.6 us (29%)
  local copies, waits for them, and re-layouts  24.9 us (18%)
  waiting for transfers between devices  24.6 us (18%)
  other arithmetic  5.88 us (4%)
    unnamed x50, local copies, waits for them, and re-layouts  19.4 us
    ppermute x7, starting transfers between devices, shift(): lax.ppermute(array, axes, [(i, (i + by) % peers) for i in range(peers)])  19.1 us
    pallas_call x1, Pallas kernels, table_of(): pl.pallas_call(table_kernel, out_shape=jax.ShapeDtypeStruct((ROWS // 256...  14.1 us
    all_to_all x2, starting transfers between devices, shared_sum(): return jnp.sum(lax.all_to_all(copies, axes, 0, 0, tiled=True), axis=0)  10.9 us
    pallas_call x1, Pallas kernels, bias_of(): pl.pallas_call(bias_kernel, out_shape=jax.ShapeDtypeStruct((HEADS, WIN, W...  10.9 us
    pallas_call x1, Pallas kernels, forward(): pl.pallas_call(forward_kernel, out_shape=(jax.ShapeDtypeStruct((WIN, D),...  8.83 us
    ppermute x3, waiting for transfers between devices, reduce_out(): total = total + lax.ppermute(piece, ('xh', 'xl'), pairs).astype(F32)  8.13 us
    all_to_all x1, waiting for transfers between devices, reduce_out(): pieces = lax.all_to_all(partial, 'z', 0, 0, tiled=True)  5.43 us
  transfers between devices with their start and end apart: 17, of which 6 were waited for; matrix products, arithmetic and copies ran while one was open for 6% of the time, Pallas kernels for 22%

profile of v1, /device:TPU:1, one launch (start us, length us, event | category | flops | bytes accessed | tf_op | source)
XLA Modules:
  0.0 137.1 jit_solution(1528356361145140034)
XLA Ops:
  0.6 1.0 copy.29.tok
  1.7 0.0 copy-start.1
  1.7 1.2 copy.30.cot
  2.9 0.9 pack.1
  3.8 9.8 %collective-permute-start = (bf16[72,1024]{1,0:T(8,128)(2,1)}, bf16[72,1024]{1,0:T(8,128)(2,1)S(1)}, u32[]{:S(2)}, u32[]{:S(2)}) collective-permute-start(bf16[72,1024]{1,0:T(8,128)(2,1)} %get-tuple-element.19), channel_id=1, source_target_pairs={{0,63},{1,0},{2,1},{3,2},{4,3},{5,4},{6,5},{7,6},{8,7},{9,8},{10,9... | collective-permute-start | bytes 442376 | tf_op jit(solution)/shard_map/ppermute | solution.py:365
  13.5 1.0 collective-permute-start.1
  14.5 1.7 %collective-permute-start.2 = (bf16[72,1024]{1,0:T(8,128)(2,1)}, bf16[72,1024]{1,0:T(8,128)(2,1)S(1)}, u32[]{:S(2)}, u32[]{:S(2)}) collective-permute-start(bf16[72,1024]{1,0:T(8,128)(2,1)} %get-tuple-element.21), channel_id=1, source_target_pairs={{0,255},{1,192},{2,193},{3,194},{4,195},{5,196},{6,197},{7,198},{8... | collective-permute-start | bytes 442376 | tf_op jit(solution)/shard_map/ppermute | solution.py:375
  16.2 0.9 pad.9.rel
  17.2 10.9 %bias.1 = f32[16,144,144]{2,1,0:T(8,128)S(1)} custom-call(s32[1]{0:T(128)} %bitcast.last, f32[16,768]{1,0:T(8,128)S(1)} %pad.8.table, s32[144,256]{1,0:T(8,128)S(1)} %pad.9.rel), custom_call_target="tpu_custom_call" | custom-call | flops 10000000 | bytes 4000000 | tf_op jit(solution)/shard_map/bias/pallas_call | solution.py:115
  28.1 0.0 copy-start.13
  28.1 0.7 copy-done.13
  28.7 0.7 copy-done.15
  29.4 0.9 copy-done.14
  30.3 0.9 copy-done.16
  31.2 8.8 %forward.1 = (bf16[144,1024]{1,0:T(8,128)(2,1)S(1)}, bf16[2,144,512]{2,1,0:T(8,128)(2,1)S(1)}, bf16[3,144,1024]{2,1,0:T(8,128)(2,1)S(1)}, bf16[144,1024]{1,0:T(8...) custom-call(bf16[2,6,12,1024]{3,2,1,0:T(8,128)(2,1)S(1)} %copy.29.to, ...), custom_call_target="tpu_custom_call" | custom-call | flops 3000000000 | bytes 24000000 | tf_op jit(solution)/shard_map/forward/pallas_call | solution.py:201
  40.1 1.0 copy-done.2
  41.1 1.0 copy-done.4
  42.1 1.0 copy-done.6
  43.0 0.8 copy-done.8
  43.9 0.7 copy-done.10
  44.6 0.7 copy-done.12
  45.3 0.6 copy-done.17
  45.9 1.4 %copy-done.19 = f32[16,144,144]{2,1,0:T(8,128)} copy-done((f32[16,144,144]{2,1,0:T(8,128)}, f32[16,144,144]{2,1,0:T(8,128)S(1)}, u32[]{:S(2)}) %copy-start.19) | copy-done | bytes 1327128
  47.4 0.5 collective-permute-start.6
  47.8 1.0 dynamic-slice_bitcast_fusion.4
  48.8 0.1 collective-permute-start.7
  49.0 1.3 collective-permute-done.7
  50.3 0.7 convolution_convert_fusion
  51.1 0.1 dynamic-slice_bitcast_fusion.2
  51.1 0.1 collective-permute-start.10
  51.2 1.5 %collective-permute-start.8 = (bf16[8,32,512]{2,1,0:T(8,128)(2,1)S(1)}, bf16[8,32,512]{2,1,0:T(8,128)(2,1)S(1)}, u32[]{:S(2)}, u32[]{:S(2)}) collective-permute-start(bf16[8,32,512]{2,1,0:T(8,128)(2,1)S(1)} %get-tuple-element.47), channel_id=1, source_target_pairs={{0,2},{2,4},{4,6},{6,0},{1,3},{3,5},{5,7},{7,1},{8,10},{10,12},{12... | collective-permute-start | bytes 786440 | tf_op jit(solution)/shard_map/ppermute | solution.py:365
  52.7 0.0 collective-permute-start.9
  52.7 14.1 %table.1 = f32[48,256]{1,0:T(8,128)S(1)} custom-call(f32[16,144,144]{2,1,0:T(8,128)S(1)} %copy-done.20, s32[144,256]{1,0:T(8,128)S(1)} %pad.9.rel), custom_call_target="tpu_custom_call" | custom-call | flops 3000000000 | bytes 4000000 | tf_op jit(solution)/shard_map/table/pallas_call | solution.py:259
  66.8 1.0 broadcast_in_dim.4
  67.8 6.6 %all-to-all-start.1 = ((f32[16,48,256]{2,1,0:T(8,128)}), f32[16,48,256]{2,1,0:T(8,128)}, u32[]{:S(2)}, u32[]{:S(2)}) async-start(f32[16,48,256]{2,1,0:T(8,128)} %broadcast_in_dim.4), calls=%async_computation.1 | async-start | bytes 1572864 | tf_op jit(solution)/shard_map/all_to_all | solution.py:385
  74.5 0.1 fusion.5
  74.6 0.1 reshape.40
  74.7 0.6 constant_dynamic-slice_fusion.2
  75.4 1.5 %collective-permute-start.11 = (bf16[8,16,256]{2,1,0:T(8,128)(2,1)S(1)}, bf16[8,16,256]{2,1,0:T(8,128)(2,1)S(1)}, u32[]{:S(2)}, u32[]{:S(2)}) collective-permute-start(bf16[8,16,256]{2,1,0:T(8,128)(2,1)S(1)} %bitcast.45), channel_id=1, source_target_pairs={{0,1},{1,0},{128,129},{129,128},{2,3},{3,2},{130,131},{131,130},{4... | collective-permute-start | bytes 196616 | tf_op jit(solution)/shard_map/ppermute | solution.py:409
  76.8 0.7 collective-permute-start.12
  77.6 1.9 %collective-permute-start.13 = (bf16[8,16,256]{2,1,0:T(8,128)(2,1)S(1)}, bf16[8,16,256]{2,1,0:T(8,128)(2,1)S(1)}, u32[]{:S(2)}, u32[]{:S(2)}) collective-permute-start(bf16[8,16,256]{2,1,0:T(8,128)(2,1)S(1)} %bitcast.47), channel_id=1, source_target_pairs={{0,129},{1,128},{128,1},{129,0},{2,131},{3,130},{130,3},{131,2},{4... | collective-permute-start | bytes 196616 | tf_op jit(solution)/shard_map/ppermute | solution.py:409
  79.5 7.2 %collective-permute-done.11 = bf16[8,16,256]{2,1,0:T(8,128)(2,1)S(1)} collective-permute-done((bf16[8,16,256]{2,1,0:T(8,128)(2,1)S(1)}, bf16[8,16,256]{2,1,0:T(8,128)(2,1)S(1)}, u32[]{:S(2)}, u32[]{:S(2)}) %collective-permute-start.11) | collective-permute-done | bytes 65568 | tf_op jit(solution)/shard_map/ppermute | solution.py:409
  86.7 0.9 collective-permute-done.12
  87.6 0.7 fusion.11
  88.3 4.0 %all-to-all-start = ((bf16[8,16,256]{2,1,0:T(8,128)(2,1)}), bf16[8,16,256]{2,1,0:T(8,128)(2,1)}, u32[]{:S(2)}, u32[]{:S(2)}) async-start(bf16[8,16,256]{2,1,0:T(8,128)(2,1)} %fusion.11), calls=%async_computation | async-start | bytes 131072 | tf_op jit(solution)/shard_map/all_to_all | solution.py:412
  92.3 1.8 %reduce_sum.28 = f32[48,256]{1,0:T(8,128)} reduce(f32[16,48,256]{2,1,0:T(8,128)} %all-to-all-done.1, f32[]{:T(128)} %constant.174.clone.1), dimensions={0}, to_apply=%region_1.2 | reduce | flops 184320 | bytes 835588 | tf_op jit(solution)/shard_map/reduce_sum | solution.py:385
  94.1 5.4 %all-to-all-done = bf16[8,16,256]{2,1,0:T(8,128)(2,1)} async-done(((bf16[8,16,256]{2,1,0:T(8,128)(2,1)}), bf16[8,16,256]{2,1,0:T(8,128)(2,1)}, u32[]{:S(2)}, u32[]{:S(2)}) %all-to-all-start) | async-done | bytes 65568 | tf_op jit(solution)/shard_map/all_to_all | solution.py:412
  99.5 1.8 %broadcast_in_dim.5 = f32[16,48,256]{2,1,0:T(8,128)} broadcast(f32[48,256]{1,0:T(8,128)} %reduce_sum.28), dimensions={1,2} | broadcast | bytes 835584 | tf_op jit(solution)/shard_map/broadcast_in_dim | solution.py:384
  101.3 4.3 %all-to-all-start.2 = ((f32[16,48,256]{2,1,0:T(8,128)}), f32[16,48,256]{2,1,0:T(8,128)}, u32[]{:S(2)}, u32[]{:S(2)}) async-start(f32[16,48,256]{2,1,0:T(8,128)} %broadcast_in_dim.5), calls=%async_computation.2 | async-start | bytes 1572864 | tf_op jit(solution)/shard_map/all_to_all | solution.py:385
  105.6 0.0 copy-start
  105.6 2.8 %copy-done = bf16[1024,3072]{1,0:T(8,128)(2,1)S(1)} copy-done((bf16[1024,3072]{1,0:T(8,128)(2,1)S(1)}, bf16[1024,3072]{1,0:T(8,128)(2,1)}, u32[]{:S(2)}) %copy-start) | copy-done | bytes 6291480
  108.4 1.1 copy-done.9
  109.5 1.0 copy-done.11
  110.4 0.9 copy-done.18
  111.3 4.7 %backward.1 = (bf16[36,1024]{1,0:T(8,128)(2,1)S(1)}, bf16[36,1024]{1,0:T(8,128)(2,1)S(1)}, bf16[36,1024]{1,0:T(8,128)(2,1)S(1)}, bf16[36,1024]{1,0:T(8,128)(2,1)S(1)}) custom-call(bf16[16,144,144]{2,1,0:T(8,128)(2,1)S(1)} %copy-done.3, bf16[16,144,144]{2,1,0:T(8,128)(2,1)S(1)} %copy-done.5, bf16[3,144,1024]{2,1,0:T(8,128)(2,1)S(1)} %copy-done.7, ...), custom_call_target="tpu_custom_call" | custom-call | flops 2000000000 | bytes 16000000 | tf_op jit(solution)/shard_map/backward/pallas_call | solution.py:319
  116.0 0.9 collective-permute-start.3
  117.0 5.9 %collective-permute-start.4 = (bf16[36,1024]{1,0:T(8,128)(2,1)S(1)}, bf16[36,1024]{1,0:T(8,128)(2,1)S(1)}, u32[]{:S(2)}, u32[]{:S(2)}) collective-permute-start(bf16[36,1024]{1,0:T(8,128)(2,1)S(1)} %get-tuple-element.31), channel_id=1, source_target_pairs={{0,64},{64,128},{128,192},{192,0},{1,65},{65,129},{129,193},{193,1... | collective-permute-start | bytes 221192 | tf_op jit(solution)/shard_map/ppermute | solution.py:365
  122.9 5.0 %collective-permute-done.3.lon = bf16[36,1024]{1,0:T(8,128)(2,1)S(1)} collective-permute-done((bf16[36,1024]{1,0:T(8,128)(2,1)S(1)}, bf16[36,1024]{1,0:T(8,128)(2,1)S(1)}, u32[]{:S(2)}, u32[]{:S(2)}) %collective-permute-start.3) | collective-permute-done | bytes 73760 | tf_op jit(solution)/shard_map/ppermute | solution.py:365
  127.8 4.8 %collective-permute-done.5.dia = bf16[36,1024]{1,0:T(8,128)(2,1)S(1)} collective-permute-done((bf16[36,1024]{1,0:T(8,128)(2,1)S(1)}, bf16[36,1024]{1,0:T(8,128)(2,1)S(1)}, u32[]{:S(2)}, u32[]{:S(2)}) %collective-permute-start.5) | collective-permute-done | bytes 73760 | tf_op jit(solution)/shard_map/ppermute | solution.py:375
  132.6 0.2 join.1
  132.8 1.0 copy.33
  133.9 1.5 %convert_reduce_fusion = f32[16,256]{1,0:T(8,128)} fusion(bf16[8,16,256]{2,1,0:T(8,128)(2,1)} %all-to-all-done), kind=kLoop, calls=%fused_computation.20 | loop fusion | flops 61440 | bytes 81920 | tf_op jit(solution)/shard_map/reduce_sum | solution.py:413
  135.3 1.2 reduce_sum.29
  136.5 0.6 copy.39
  (41 shorter events, 0.1 us)
Async XLA Ops:
  0.6 16.5 %copy-start.21 = (f32[759,16]{0,1:T(8,128)S(1)}, f32[759,16]{0,1:T(8,128)}, u32[]{:S(2)}) copy-start(f32[759,16]{0,1:T(8,128)} %param.10) | copy-start | bytes 145732
  1.7 27.7 %copy-start.1 = (bf16[1024,1024]{1,0:T(8,128)(2,1)S(1)}, bf16[1024,1024]{1,0:T(8,128)(2,1)}, u32[]{:S(2)}) copy-start(bf16[1024,1024]{1,0:T(8,128)(2,1)} %wout_hbm.1) | copy-start | bytes 6291460
  3.8 24.3 %collective-permute-start = (bf16[72,1024]{1,0:T(8,128)(2,1)}, bf16[72,1024]{1,0:T(8,128)(2,1)S(1)}, u32[]{:S(2)}, u32[]{:S(2)}) collective-permute-start(bf16[72,1024]{1,0:T(8,128)(2,1)} %get-tuple-element.19), channel_id=1, source_target_pairs={{0,63},{1,0},{2,1},{3,2},{4,3},{5,4},{6,5},{7,6},{8,7},{9,8},{10,9... | collective-permute-start | bytes 442376 | tf_op jit(solution)/shard_map/ppermute | solution.py:365
  13.5 14.5 %collective-permute-start.1 = (bf16[72,1024]{1,0:T(8,128)(2,1)}, bf16[72,1024]{1,0:T(8,128)(2,1)S(1)}, u32[]{:S(2)}, u32[]{:S(2)}) collective-permute-start(bf16[72,1024]{1,0:T(8,128)(2,1)} %get-tuple-element.20), channel_id=1, source_target_pairs={{0,192},{64,0},{128,64},{192,128},{1,193},{65,1},{129,65},{193,129... | collective-permute-start | bytes 442376 | tf_op jit(solution)/shard_map/ppermute | solution.py:365
  14.5 14.2 %collective-permute-start.2 = (bf16[72,1024]{1,0:T(8,128)(2,1)}, bf16[72,1024]{1,0:T(8,128)(2,1)S(1)}, u32[]{:S(2)}, u32[]{:S(2)}) collective-permute-start(bf16[72,1024]{1,0:T(8,128)(2,1)} %get-tuple-element.21), channel_id=1, source_target_pairs={{0,255},{1,192},{2,193},{3,194},{4,195},{5,196},{6,197},{7,198},{8... | collective-permute-start | bytes 442376 | tf_op jit(solution)/shard_map/ppermute | solution.py:375
  28.1 0.7 copy-start.13
  28.7 0.7 copy-start.15
  29.4 0.9 copy-start.14
  30.3 0.9 copy-start.16
  40.1 1.0 copy-start.2
  41.1 1.0 copy-start.4
  42.1 1.0 copy-start.6
  43.0 0.8 copy-start.8
  43.9 0.7 copy-start.10
  44.6 0.7 copy-start.12
  45.3 0.6 copy-start.17
  45.9 1.4 %copy-start.19 = (f32[16,144,144]{2,1,0:T(8,128)}, f32[16,144,144]{2,1,0:T(8,128)S(1)}, u32[]{:S(2)}) copy-start(f32[16,144,144]{2,1,0:T(8,128)S(1)} %get-tuple-element.34.grads) | copy-start | bytes 3981316
  47.4 3.0 %collective-permute-start.6 = (bf16[144,1024]{1,0:T(8,128)(2,1)S(1)}, bf16[144,1024]{1,0:T(8,128)(2,1)S(1)}, u32[]{:S(2)}, u32[]{:S(2)}) collective-permute-start(bf16[144,1024]{1,0:T(8,128)(2,1)S(1)} %get-tuple-element.26.cot), channel_id=1, source_target_pairs={{0,64},{64,0},{1,65},{65,1},{2,66},{66,2},{3,67},{67,3},{4,68},{68... | collective-permute-start | bytes 884744 | tf_op jit(solution)/shard_map/ppermute | solution.py:391
  48.8 1.5 %collective-permute-start.7 = (bf16[144,512]{1,0:T(8,128)(2,1)S(1)}, bf16[144,512]{1,0:T(8,128)(2,1)S(1)}, u32[]{:S(2)}, u32[]{:S(2)}) collective-permute-start(bf16[144,512]{1,0:T(8,128)(2,1)S(1)} %get-tuple-element.51), channel_id=1, source_target_pairs={{0,64},{64,0},{1,65},{65,1},{2,66},{66,2},{3,67},{67,3},{4,68},{68... | collective-permute-start | bytes 442376 | tf_op jit(solution)/shard_map/ppermute | solution.py:390
  50.3 2.4 %copy-start.20 = (f32[16,144,144]{2,1,0:T(8,128)S(1)}, f32[16,144,144]{2,1,0:T(8,128)}, u32[]{:S(2)}) copy-start(f32[16,144,144]{2,1,0:T(8,128)} %copy-done.19) | copy-start | bytes 3981316
  51.1 23.3 %collective-permute-start.10 = (bf16[8,32,512]{2,1,0:T(8,128)(2,1)S(1)}, bf16[8,32,512]{2,1,0:T(8,128)(2,1)S(1)}, u32[]{:S(2)}, u32[]{:S(2)}) collective-permute-start(bf16[8,32,512]{2,1,0:T(8,128)(2,1)S(1)} %get-tuple-element.48), channel_id=1, source_target_pairs={{0,6},{2,0},{4,2},{6,4},{1,7},{3,1},{5,3},{7,5},{8,14},{10,8},{12,... | collective-permute-start | bytes 786440 | tf_op jit(solution)/shard_map/ppermute | solution.py:365
  51.2 23.2 %collective-permute-start.8 = (bf16[8,32,512]{2,1,0:T(8,128)(2,1)S(1)}, bf16[8,32,512]{2,1,0:T(8,128)(2,1)S(1)}, u32[]{:S(2)}, u32[]{:S(2)}) collective-permute-start(bf16[8,32,512]{2,1,0:T(8,128)(2,1)S(1)} %get-tuple-element.47), channel_id=1, source_target_pairs={{0,2},{2,4},{4,6},{6,0},{1,3},{3,5},{5,7},{7,1},{8,10},{10,12},{12... | collective-permute-start | bytes 786440 | tf_op jit(solution)/shard_map/ppermute | solution.py:365
  52.7 21.8 %collective-permute-start.9 = (bf16[8,32,512]{2,1,0:T(8,128)(2,1)S(1)}, bf16[8,32,512]{2,1,0:T(8,128)(2,1)S(1)}, u32[]{:S(2)}, u32[]{:S(2)}) collective-permute-start(bf16[8,32,512]{2,1,0:T(8,128)(2,1)S(1)} %get-tuple-element.49), channel_id=1, source_target_pairs={{0,4},{2,6},{4,0},{6,2},{1,5},{3,7},{5,1},{7,3},{8,12},{10,14},{12... | collective-permute-start | bytes 786440 | tf_op jit(solution)/shard_map/ppermute | solution.py:365
  67.8 20.5 %all-to-all-start.1 = ((f32[16,48,256]{2,1,0:T(8,128)}), f32[16,48,256]{2,1,0:T(8,128)}, u32[]{:S(2)}, u32[]{:S(2)}) async-start(f32[16,48,256]{2,1,0:T(8,128)} %broadcast_in_dim.4), calls=%async_computation.1 | async-start | bytes 1572864 | tf_op jit(solution)/shard_map/all_to_all | solution.py:385
  75.3 30.3 %copy-start.3 = (bf16[16,144,144]{2,1,0:T(8,128)(2,1)S(1)}, bf16[16,144,144]{2,1,0:T(8,128)(2,1)}, u32[]{:S(2)}) copy-start(bf16[16,144,144]{2,1,0:T(8,128)(2,1)} %copy-done.2) | copy-start | bytes 1990660
  75.3 30.3 %copy-start.5 = (bf16[16,144,144]{2,1,0:T(8,128)(2,1)S(1)}, bf16[16,144,144]{2,1,0:T(8,128)(2,1)}, u32[]{:S(2)}) copy-start(bf16[16,144,144]{2,1,0:T(8,128)(2,1)} %copy-done.4) | copy-start | bytes 1990660
  75.3 30.3 %copy-start.7 = (bf16[3,144,1024]{2,1,0:T(8,128)(2,1)S(1)}, bf16[3,144,1024]{2,1,0:T(8,128)(2,1)}, u32[]{:S(2)}) copy-start(bf16[3,144,1024]{2,1,0:T(8,128)(2,1)} %copy-done.6) | copy-start | bytes 2654212
  75.4 11.4 %collective-permute-start.11 = (bf16[8,16,256]{2,1,0:T(8,128)(2,1)S(1)}, bf16[8,16,256]{2,1,0:T(8,128)(2,1)S(1)}, u32[]{:S(2)}, u32[]{:S(2)}) collective-permute-start(bf16[8,16,256]{2,1,0:T(8,128)(2,1)S(1)} %bitcast.45), channel_id=1, source_target_pairs={{0,1},{1,0},{128,129},{129,128},{2,3},{3,2},{130,131},{131,130},{4... | collective-permute-start | bytes 196616 | tf_op jit(solution)/shard_map/ppermute | solution.py:409
  76.8 10.8 %collective-permute-start.12 = (bf16[8,16,256]{2,1,0:T(8,128)(2,1)S(1)}, bf16[8,16,256]{2,1,0:T(8,128)(2,1)S(1)}, u32[]{:S(2)}, u32[]{:S(2)}) collective-permute-start(bf16[8,16,256]{2,1,0:T(8,128)(2,1)S(1)} %bitcast.46), channel_id=1, source_target_pairs={{0,128},{1,129},{128,0},{129,1},{2,130},{3,131},{130,2},{131,3},{4... | collective-permute-start | bytes 196616 | tf_op jit(solution)/shard_map/ppermute | solution.py:409
  77.6 10.0 %collective-permute-start.13 = (bf16[8,16,256]{2,1,0:T(8,128)(2,1)S(1)}, bf16[8,16,256]{2,1,0:T(8,128)(2,1)S(1)}, u32[]{:S(2)}, u32[]{:S(2)}) collective-permute-start(bf16[8,16,256]{2,1,0:T(8,128)(2,1)S(1)} %bitcast.47), channel_id=1, source_target_pairs={{0,129},{1,128},{128,1},{129,0},{2,131},{3,130},{130,3},{131,2},{4... | collective-permute-start | bytes 196616 | tf_op jit(solution)/shard_map/ppermute | solution.py:409
  88.3 11.2 %all-to-all-start = ((bf16[8,16,256]{2,1,0:T(8,128)(2,1)}), bf16[8,16,256]{2,1,0:T(8,128)(2,1)}, u32[]{:S(2)}, u32[]{:S(2)}) async-start(bf16[8,16,256]{2,1,0:T(8,128)(2,1)} %fusion.11), calls=%async_computation | async-start | bytes 131072 | tf_op jit(solution)/shard_map/all_to_all | solution.py:412
  101.3 34.0 %all-to-all-start.2 = ((f32[16,48,256]{2,1,0:T(8,128)}), f32[16,48,256]{2,1,0:T(8,128)}, u32[]{:S(2)}, u32[]{:S(2)}) async-start(f32[16,48,256]{2,1,0:T(8,128)} %broadcast_in_dim.5), calls=%async_computation.2 | async-start | bytes 1572864 | tf_op jit(solution)/shard_map/all_to_all | solution.py:385
  105.6 2.8 %copy-start = (bf16[1024,3072]{1,0:T(8,128)(2,1)S(1)}, bf16[1024,3072]{1,0:T(8,128)(2,1)}, u32[]{:S(2)}) copy-start(bf16[1024,3072]{1,0:T(8,128)(2,1)} %wqkv_hbm.3) | copy-start | bytes 18874372
  108.4 1.1 copy-start.9
  109.5 1.0 copy-start.11
  110.4 0.9 copy-start.18
  116.0 11.8 %collective-permute-start.3 = (bf16[36,1024]{1,0:T(8,128)(2,1)S(1)}, bf16[36,1024]{1,0:T(8,128)(2,1)S(1)}, u32[]{:S(2)}, u32[]{:S(2)}) collective-permute-start(bf16[36,1024]{1,0:T(8,128)(2,1)S(1)} %get-tuple-element.30), channel_id=1, source_target_pairs={{0,1},{1,2},{2,3},{3,4},{4,5},{5,6},{6,7},{7,8},{8,9},{9,10},{10,1... | collective-permute-start | bytes 221192 | tf_op jit(solution)/shard_map/ppermute | solution.py:365
  117.0 10.9 %collective-permute-start.4 = (bf16[36,1024]{1,0:T(8,128)(2,1)S(1)}, bf16[36,1024]{1,0:T(8,128)(2,1)S(1)}, u32[]{:S(2)}, u32[]{:S(2)}) collective-permute-start(bf16[36,1024]{1,0:T(8,128)(2,1)S(1)} %get-tuple-element.31), channel_id=1, source_target_pairs={{0,64},{64,128},{128,192},{192,0},{1,65},{65,129},{129,193},{193,1... | collective-permute-start | bytes 221192 | tf_op jit(solution)/shard_map/ppermute | solution.py:365
  122.9 9.7 %collective-permute-start.5 = (bf16[36,1024]{1,0:T(8,128)(2,1)S(1)}, bf16[36,1024]{1,0:T(8,128)(2,1)S(1)}, u32[]{:S(2)}, u32[]{:S(2)}) collective-permute-start(bf16[36,1024]{1,0:T(8,128)(2,1)S(1)} %get-tuple-element.32), channel_id=1, source_target_pairs={{0,65},{1,66},{2,67},{3,68},{4,69},{5,70},{6,71},{7,72},{8,73},{9,... | collective-permute-start | bytes 221192 | tf_op jit(solution)/shard_map/ppermute | solution.py:375
